TPU v7x, 32 devices: a whole 2x2x4 slice. The times are simulated.
32 devices in a mesh: grp: 2 (over x), ex: 4 (over y, core), feat: 4 (over z).
Axes of the slice: x: 2, y: 2, z: 4, core: 2. Of those that a mesh axis runs over, the one named last changes fastest.
Arguments:
- queries: bfloat16 [640, 16384], P(('grp', 'ex'), 'feat'), parts along dimension 0, may hold values from -6 to 6
- train_grads: bfloat16 [8192, 16384], P(('grp', 'ex'), 'feat'), parts along dimension 0, may hold values from -6 to 6
- preconditioner: bfloat16 [8, 2048, 2048], P('feat', 'ex'), as said below
- query_ids: int32 [640], P(('grp', 'feat')), parts along dimension 0, may hold values from 0 to 4095
- train_ids: int32 [8192], P(('grp', 'ex')), parts along dimension 0, may hold values from 0 to 4095, each once
- layer_seeds: int32 [8], P('feat'), may hold values from 0 to 1073741823
Outputs:
- scores: float32 [640, 4096], P(('grp', 'feat'), 'ex'), parts along dimension 0
There are 2 independent parts, one for each index of `grp`. A program takes and returns all parts, laid end to end along the dimension named above; an argument that names none is the same for every part. Nothing has to cross between parts.
Inputs may be any that keep to these rules, and one draw needn't show every extreme that they name: preconditioner[l] is symmetric for every layer. `train_ids`: each training example id appears once in the slab. `query_ids`: every query id is the id of some training example of the slab.
All inputs are finite; a program needn't handle non-finite values.
Results may differ from a plain program's by a relative error of at most 0.003.
Values may be sent and summed in bfloat16 or wider, within the bound.
A program may use at most 128 MiB of HBM per device.

v0:
```python
import math

import jax
import jax.numpy as jnp
from jax import lax
from jax.sharding import PartitionSpec as P


def sketch_signs(seed_values, feature_count):
    feature_index = jnp.arange(feature_count, dtype=jnp.int32)
    hashed = seed_values[:, None] + feature_index[None, :] * 40503
    hashed = (hashed ^ lax.shift_right_logical(hashed, jnp.full_like(hashed, 16))) * 73244475
    hashed = (hashed ^ lax.shift_right_logical(hashed, jnp.full_like(hashed, 16))) * 73244475
    hashed = hashed ^ lax.shift_right_logical(hashed, jnp.full_like(hashed, 16))
    return 1 - 2 * (hashed & 1)


def local(queries, train_grads, preconditioner, query_ids, train_ids, layer_seeds):
    lay_count, row_block, layer_width = preconditioner.shape
    sign_flips = sketch_signs(layer_seeds, layer_width).reshape(-1).astype(jnp.bfloat16)
    signed_rows = queries * sign_flips[None, :]
    all_signed = lax.all_gather(signed_rows, "ex", axis=0, tiled=True)
    layered = all_signed.reshape(all_signed.shape[0], lay_count, layer_width)
    column_part = jnp.einsum(
        "qlj,lcj->qlc", layered, preconditioner, preferred_element_type=jnp.float32
    ).astype(jnp.bfloat16)
    joined = lax.all_gather(column_part, "ex", axis=2, tiled=True)
    everyone = joined.reshape(joined.shape[0], lay_count * layer_width)
    feat_count = lax.axis_size("feat")
    summed = lax.psum_scatter(
        jnp.einsum("qf,tf->qt", everyone, train_grads, preferred_element_type=jnp.float32),
        "feat",
        scatter_dimension=0,
        tiled=True,
    )
    normal = 1.0 / math.sqrt(feat_count * lay_count * layer_width)
    scaled = summed * normal
    return jnp.where(query_ids[:, None] == train_ids[None, :], jnp.float32(0.0), scaled)


def solution(mesh):
    in_specs = (
        P(("grp", "ex"), "feat"),
        P(("grp", "ex"), "feat"),
        P("feat", "ex", None),
        P(("grp", "feat")),
        P(("grp", "ex")),
        P("feat"),
    )
    out_specs = P(("grp", "feat"), "ex")
    return jax.shard_map(local, mesh=mesh, in_specs=in_specs, out_specs=out_specs, check_vma=False)
```

profile of v0, /device:TPU:0, one launch (start us, length us, event | category | flops | bytes accessed | tf_op | source)
XLA Modules:
  0.0 118.0 jit_solution(12641282813158469454)
XLA Ops:
  6.5 0.0 all-gather.3.cloned.1.call-start
  6.5 0.7 add_bitcast_fusion
  7.3 2.0 %broadcast_multiply_fusion = bf16[80,4096]{1,0:T(8,128)(2,1)} fusion(bf16[80,4096]{1,0:T(8,128)(2,1)} %param.6, bf16[4096]{0:T(1024)(128)(2,1)S(1)} %fusion.14), kind=kLoop, calls=%fused_computation.6 | loop fusion | flops 327680 | bytes 1318912 | tf_op jit(solution)/shard_map/mul | solution.py:21
  9.3 0.0 all-gather.3.cloned.1.call-update
  9.3 0.0 all-gather.5.cloned.1.call-start
  9.4 28.4 %all-gather.3.cloned.1.call-done = bf16[320,4096]{1,0:T(8,128)(2,1)} async-done(((bf16[80,4096]{1,0:T(8,128)(2,1)}), bf16[320,4096]{1,0:T(8,128)(2,1)}) %all-gather.3.cloned.1.call-update) | async-done | bytes 2621456 | tf_op jit(solution)/shard_map/all_gather | solution.py:22
  37.7 5.4 %fusion.6 = bf16[320,2,512]{2,0,1:T(8,128)(2,1)} fusion(bf16[2,512,2048]{2,1,0:T(8,128)(2,1)} %param.8, bf16[40,2,8,2048]{3,2,1,0:T(8,128)(2,1)} %bitcast.21), kind=kOutput, calls=%fused_computation.4 | convolution fusion | flops 1342504960 | bytes 7471104 | tf_op jit(solution)/shard_map/qlj,lcj->qlc/dot_general | solution.py:24
  43.1 0.0 all-gather.5.cloned.1.call-update
  43.1 0.0 reduce-scatter.2.cloned.1.call-start
  43.2 25.7 %all-gather.5.cloned.1.call-done = bf16[320,2,2048]{2,0,1:T(8,128)(2,1)} async-done(((bf16[320,2,512]{2,0,1:T(8,128)(2,1)}), bf16[320,2,2048]{2,0,1:T(8,128)(2,1)}) %all-gather.5.cloned.1.call-update) | async-done | bytes 2621456 | tf_op jit(solution)/shard_map/all_gather | solution.py:27
  68.8 2.1 %copy.10 = bf16[2,40,8,2048]{3,2,0,1:T(8,128)(2,1)S(1)} copy(bf16[2,40,8,2048]{3,2,1,0:T(8,128)(2,1)} %bitcast.18) | data formatting | bytes 5242880 | tf_op jit(solution)/shard_map/reshape | solution.py:28
  70.9 0.0 copy-start
  70.9 0.0 copy-start.1
  70.9 7.4 %fusion.15 = f32[320,1024]{1,0:T(8,128)} fusion(bf16[320,4096]{1,0:T(8,128)(2,1)S(1)} %bitcast.19, bf16[1024,4096]{1,0:T(8,128)(2,1)} %param.7), kind=kOutput, calls=%fused_computation.18 | convolution fusion | flops 2684354560 | bytes 12320768 | tf_op jit(solution)/shard_map/qf,tf->qt/dot_general | solution.py:31
  78.3 0.0 reduce-scatter.2.cloned.1.call-update
  78.3 31.4 %reduce-scatter.2.cloned.1.call-done = f32[80,1024]{1,0:T(8,128)} async-done(((f32[320,1024]{1,0:T(8,128)}), f32[80,1024]{1,0:T(8,128)}) %reduce-scatter.2.cloned.1.call-update) | async-done | bytes 327696 | tf_op jit(solution)/shard_map/reduce_scatter | solution.py:30
  109.7 0.0 copy-done
  109.7 0.0 copy-done.1
  109.7 1.8 %multiply_select_fusion = f32[80,1024]{1,0:T(8,128)} fusion(f32[80,1024]{1,0:T(8,128)} %reduce-scatter.2.cloned.1.call-done, s32[1024]{0:T(1024)S(1)} %copy-done, s32[80]{0:T(128)S(1)} %copy-done.1), kind=kLoop, calls=%fused_computation.5 | loop fusion | flops 245760 | bytes 659776 | tf_op jit(solution)/shard_map/jit(_where)/select_n | solution.py:38
  (3 shorter events, 0.0 us)
Async XLA Ops:
  6.5 31.2 %all-gather.3.cloned.1.call-start = ((), (), s32[]{:S(2)}) async-start(), calls=%async_computation.1 | async-start | bytes 3276800 | tf_op jit(solution)/shard_map/all_gather | solution.py:22
  9.3 59.5 %all-gather.5.cloned.1.call-start = ((), (), s32[]{:S(2)}) async-start(), calls=%async_computation.2 | async-start | bytes 3276800 | tf_op jit(solution)/shard_map/all_gather | solution.py:27
  43.1 66.6 %reduce-scatter.2.cloned.1.call-start = ((), (), s32[]{:S(2)}) async-start(), calls=%async_computation.3 | async-start | bytes 1638400 | tf_op jit(solution)/shard_map/reduce_scatter | solution.py:30
  70.9 38.8 %copy-start = (s32[1024]{0:T(1024)S(1)}, s32[1024]{0:T(1024)}, u32[]{:S(2)}) copy-start(s32[1024]{0:T(1024)} %param.10) | copy-start | bytes 12292
  70.9 38.8 %copy-start.1 = (s32[80]{0:T(128)S(1)}, s32[80]{0:T(128)}, u32[]{:S(2)}) copy-start(s32[80]{0:T(128)} %param.9) | copy-start | bytes 964
Sparse Core Ops, SparseCore 0:
  9.4 28.2 all-gather.2
  43.3 25.5 all-gather.4
  78.4 31.2 reduce-scatter.1
where the time goes:
time: 118 us
  waiting for transfers between devices  85.4 us (72%)
  between operations  13.1 us (11%)
  matrix products  12.7 us (11%)
  other arithmetic  4.53 us (4%)
  local copies, waits for them, and re-layouts  2.08 us (2%)
    reduce_scatter x1, waiting for transfers between devices, local(): lax.psum_scatter(jnp.einsum('qf,tf->qt', everyone, train_grads, preferred...  31.4 us
    all_gather x1, waiting for transfers between devices, local(): all_signed = lax.all_gather(signed_rows, 'ex', axis=0, tiled=True)  28.4 us
    all_gather x1, waiting for transfers between devices, local(): joined = lax.all_gather(column_part, 'ex', axis=2, tiled=True)  25.7 us
    dot_general x1, matrix products, local(): jnp.einsum('qf,tf->qt', everyone, train_grads, preferred_element_type=jnp...  7.36 us
    dot_general x1, matrix products, local(): jnp.einsum('qlj,lcj->qlc', layered, preconditioner, preferred_element_typ...  5.39 us
  transfers between devices with their start and end apart: 3, of which 3 were waited for; matrix products, arithmetic and copies ran while one was open for 0% of the time, Pallas kernels for 0%

commit v1 on v0

v1 whole, which is shorter than its diff:
```python
import functools
import math

import jax
import jax.numpy as jnp
from jax import lax
from jax.experimental import pallas as pl
from jax.experimental.pallas import tpu as pltpu
from jax.sharding import PartitionSpec as P

CHUNK = 16
TILE = 256
NT = (((1,), (1,)), ((), ()))


def sketch_sign_row(seed, width):
    feature = lax.broadcasted_iota(jnp.int32, (1, width), 1)
    hashed = seed + feature * 40503
    sixteen = jnp.full_like(hashed, 16)
    hashed = (hashed ^ lax.shift_right_logical(hashed, sixteen)) * 73244475
    hashed = (hashed ^ lax.shift_right_logical(hashed, sixteen)) * 73244475
    hashed = hashed ^ lax.shift_right_logical(hashed, sixteen)
    return (1 - 2 * (hashed & 1)).astype(jnp.float32).astype(jnp.bfloat16)


def kernel(
    n_ex, n_feat,
    q_hbm, g_hbm, p_hbm, qid_ref, tid_ref, seed_ref, out_ref,
    qbuf, cbuf, gbuf, pbuf, sbuf, zbuf, own, qcol,
    load_q, load_p, load_g,
    q_sib_s, q_sib_r, q_y_s, q_y_r, q_fw_s, q_fw_r,
    c_sib_s, c_sib_r, c_y_s, c_y_r, c_fw_s, c_fw_r,
    z_s, z_r,
):
    rows, feats = q_hbm.shape
    layers, prow, width = p_hbm.shape
    train = g_hbm.shape[0]
    steps = rows // CHUNK
    part = layers * prow
    per_owner = n_ex // n_feat
    far = n_ex // 2 - 1
    me = lax.axis_index("ex")
    fe = lax.axis_index("feat")
    sib = me + 1 - 2 * lax.rem(me, 2)

    def block(k, e):
        return qbuf.at[k, pl.ds(pl.multiple_of(e * CHUNK, CHUNK), CHUNK)]

    def columns(e):
        return pl.ds(pl.multiple_of(e * part, 128), part)

    def ahead(j):
        return lax.rem(me + 2 * j, n_ex)

    def behind(e, j):
        return lax.rem(e + n_ex - 2 * j, n_ex)

    def remote(ref, send, recv, target):
        return pltpu.make_async_remote_copy(
            src_ref=ref, dst_ref=ref, send_sem=send, recv_sem=recv,
            device_id={"ex": target}, device_id_type=pl.DeviceIdType.MESH,
        )

    q_loads = [
        pltpu.make_async_copy(q_hbm.at[pl.ds(k * CHUNK, CHUNK)], block(k, me), load_q.at[k])
        for k in range(steps)
    ]
    p_loads = [
        pltpu.make_async_copy(p_hbm.at[l], pbuf.at[l], load_p.at[l]) for l in range(layers)
    ]
    g_loads = [
        pltpu.make_async_copy(
            g_hbm.at[:, pl.ds(l * width + e * prow, prow)],
            gbuf.at[:, pl.ds(e * part + l * prow, prow)],
            load_g.at[e * layers + l],
        )
        for e in range(n_ex)
        for l in range(layers)
    ]
    for copy in q_loads + p_loads + g_loads:
        copy.start()

    barrier = pltpu.get_barrier_semaphore()
    pl.semaphore_signal(barrier, inc=1, device_id={"ex": sib}, device_id_type=pl.DeviceIdType.MESH)
    for j in range(1, far + 1):
        pl.semaphore_signal(barrier, inc=1, device_id={"ex": ahead(j)}, device_id_type=pl.DeviceIdType.MESH)
    for d in range(1, n_feat):
        pl.semaphore_signal(
            barrier, inc=1, device_id={"feat": lax.rem(fe + d, n_feat)}, device_id_type=pl.DeviceIdType.MESH
        )

    signs = [sketch_sign_row(seed_ref[l], width) for l in range(layers)]
    eye = lax.broadcasted_iota(jnp.int32, (qid_ref.shape[1],) * 2, 0) == lax.broadcasted_iota(
        jnp.int32, (qid_ref.shape[1],) * 2, 1
    )
    ids = jnp.broadcast_to(qid_ref[...].astype(jnp.float32), eye.shape)
    qcol[...] = jnp.broadcast_to(
        jnp.sum(jnp.where(eye, ids, 0.0), axis=1, keepdims=True), qcol.shape
    )

    sent = []

    def go(copy):
        copy.start()
        sent.append(copy)

    for k in range(steps):
        q_loads[k].wait()
        place = pl.ds(pl.multiple_of(me * CHUNK, CHUNK), CHUNK)
        for l in range(layers):
            lanes = slice(l * width, (l + 1) * width)
            qbuf[k, place, lanes] = qbuf[k, place, lanes] * signs[l]
        if k == 0:
            pl.semaphore_wait(barrier, far + n_feat)
        for j in range(1, far + 1):
            go(remote(block(k, me), q_y_s.at[j - 1, k], q_y_r.at[j - 1, k], ahead(j)))
        go(remote(block(k, me), q_sib_s.at[k], q_sib_r.at[k], sib))

    for k in range(steps):
        for j in range(1, far + 1):
            src = behind(me, j)
            remote(block(k, src), q_y_s.at[j - 1, k], q_y_r.at[j - 1, k], ahead(j)).wait_recv()
            go(remote(block(k, src), q_fw_s.at[j - 1, k], q_fw_r.at[j - 1, k], sib))
        remote(block(k, sib), q_sib_s.at[k], q_sib_r.at[k], sib).wait_recv()
        for j in range(1, far + 1):
            src = behind(sib, j)
            remote(block(k, src), q_fw_s.at[j - 1, k], q_fw_r.at[j - 1, k], sib).wait_recv()
        if k == 0:
            for copy in p_loads:
                copy.wait()
        for l in range(layers):
            got = lax.dot_general(
                qbuf[k, :, l * width:(l + 1) * width], pbuf[l], NT, preferred_element_type=jnp.float32
            )
            cbuf[k, :, pl.ds(pl.multiple_of(me * part + l * prow, 128), prow)] = got.astype(jnp.bfloat16)
        mine = cbuf.at[k, :, columns(me)]
        for j in range(1, far + 1):
            go(remote(mine, c_y_s.at[j - 1, k], c_y_r.at[j - 1, k], ahead(j)))
        go(remote(mine, c_sib_s.at[k], c_sib_r.at[k], sib))

    normal = 1.0 / math.sqrt(n_feat * layers * width)

    def z_copy(k, b):
        owner, spot = b // per_owner, (b % per_owner) * steps + k
        return pltpu.make_async_remote_copy(
            src_ref=sbuf.at[k, pl.ds(b * CHUNK, CHUNK)],
            dst_ref=zbuf.at[fe, pl.ds(spot * CHUNK, CHUNK)],
            send_sem=z_s.at[k, b],
            recv_sem=z_r.at[fe, spot],
            device_id={"feat": owner},
            device_id_type=pl.DeviceIdType.MESH,
        )

    def finish(k):
        for m in range(per_owner):
            spot = m * steps + k
            band = pl.ds(spot * CHUNK, CHUNK)
            total = own[band, :]
            for d in range(1, n_feat):
                src = lax.rem(fe + d, n_feat)
                pltpu.make_async_remote_copy(
                    src_ref=zbuf.at[src, band], dst_ref=zbuf.at[src, band],
                    send_sem=z_s.at[k, m], recv_sem=z_r.at[src, spot],
                    device_id={"feat": src}, device_id_type=pl.DeviceIdType.MESH,
                ).wait_recv()
                total = total + zbuf[src, band, :].astype(jnp.float32)
            same = qcol[band, 0:1] == tid_ref[...].astype(jnp.float32)
            out_ref[band, :] = jnp.where(same, 0.0, total * normal)

    for k in range(steps):
        for j in range(1, far + 1):
            got = cbuf.at[k, :, columns(behind(me, j))]
            remote(got, c_y_s.at[j - 1, k], c_y_r.at[j - 1, k], ahead(j)).wait_recv()
            go(remote(got, c_fw_s.at[j - 1, k], c_fw_r.at[j - 1, k], sib))
        remote(cbuf.at[k, :, columns(sib)], c_sib_s.at[k], c_sib_r.at[k], sib).wait_recv()
        for j in range(1, far + 1):
            got = cbuf.at[k, :, columns(behind(sib, j))]
            remote(got, c_fw_s.at[j - 1, k], c_fw_r.at[j - 1, k], sib).wait_recv()
        if k == 0:
            for copy in g_loads:
                copy.wait()

        for n in range(train // TILE):
            tile = slice(n * TILE, (n + 1) * TILE)
            scores = lax.dot_general(cbuf[k], gbuf[tile, :], NT, preferred_element_type=jnp.float32)
            sbuf[k, :, tile] = scores.astype(jnp.bfloat16)
            for b in range(n_ex):
                @pl.when(fe == b // per_owner)
                def _():
                    spot = (b % per_owner) * steps + k
                    own[spot * CHUNK:(spot + 1) * CHUNK, tile] = scores[b * CHUNK:(b + 1) * CHUNK]

        for b in range(n_ex):
            @pl.when(fe != b // per_owner)
            def _():
                z_copy(k, b).start()
        if k > 0:
            finish(k - 1)
    finish(steps - 1)

    for copy in sent:
        copy.wait_send()
    for k in range(steps):
        for b in range(n_ex):
            @pl.when(fe != b // per_owner)
            def _():
                z_copy(k, b).wait_send()


def local(n_ex, n_feat, queries, train_grads, preconditioner, query_ids, train_ids, layer_seeds):
    rows, feats = queries.shape
    layers, prow, width = preconditioner.shape
    train = train_grads.shape[0]
    out_rows = query_ids.shape[0]
    steps = rows // CHUNK
    far = max(n_ex // 2 - 1, 1)
    dma = pltpu.SemaphoreType.DMA
    any_space = pl.BlockSpec(memory_space=pl.ANY)
    vmem = pl.BlockSpec(memory_space=pltpu.VMEM)
    return pl.pallas_call(
        functools.partial(kernel, n_ex, n_feat),
        out_shape=jax.ShapeDtypeStruct((out_rows, train), jnp.float32),
        in_specs=[any_space, any_space, any_space, vmem, vmem, pl.BlockSpec(memory_space=pltpu.SMEM)],
        out_specs=vmem,
        scratch_shapes=[
            pltpu.VMEM((steps, n_ex * CHUNK, feats), jnp.bfloat16),
            pltpu.VMEM((steps, n_ex * CHUNK, feats), jnp.bfloat16),
            pltpu.VMEM((train, feats), jnp.bfloat16),
            pltpu.VMEM((layers, prow, width), jnp.bfloat16),
            pltpu.VMEM((steps, n_ex * CHUNK, train), jnp.bfloat16),
            pltpu.VMEM((n_feat, out_rows, train), jnp.bfloat16),
            pltpu.VMEM((out_rows, train), jnp.float32),
            pltpu.VMEM((out_rows, 128), jnp.float32),
            dma((steps,)), dma((layers,)), dma((n_ex * layers,)),
            dma((steps,)), dma((steps,)), dma((far, steps)), dma((far, steps)), dma((far, steps)), dma((far, steps)),
            dma((steps,)), dma((steps,)), dma((far, steps)), dma((far, steps)), dma((far, steps)), dma((far, steps)),
            dma((steps, n_ex)), dma((n_feat, steps * (n_ex // n_feat))),
        ],
        compiler_params=pltpu.CompilerParams(
            collective_id=0, has_side_effects=True, vmem_limit_bytes=56 * 1024 * 1024
        ),
        cost_estimate=pl.CostEstimate(
            flops=2 * n_ex * rows * feats * (prow + train),
            bytes_accessed=2 * feats * (rows + layers * prow // 2 + train),
            transcendentals=0,
        ),
    )(
        queries, train_grads, preconditioner,
        query_ids.reshape(1, -1), train_ids.reshape(1, -1), layer_seeds,
    )


def solution(mesh):
    in_specs = (
        P(("grp", "ex"), "feat"),
        P(("grp", "ex"), "feat"),
        P("feat", "ex", None),
        P(("grp", "feat")),
        P(("grp", "ex")),
        P("feat"),
    )
    out_specs = P(("grp", "feat"), "ex")
    body = functools.partial(local, mesh.shape["ex"], mesh.shape["feat"])
    return jax.shard_map(body, mesh=mesh, in_specs=in_specs, out_specs=out_specs, check_vma=False)
```

time: 118 us -> 64.1 us (0.54)
  waiting for transfers between devices: 85.4 us -> 0 us
  Pallas kernels: 0 us -> 62.2 us
  between operations: 13.1 us -> 0.01 us
  matrix products: 12.7 us -> 0 us
  other arithmetic: 4.53 us -> 0 us
    pallas_call x0 -> x1, Pallas kernels: none -> 62.2 us  [local(): pl.pallas_call(functools.partial(kernel, n_ex, n_feat), out_shape=jax.Sha...]
    all_gather x2 -> x0, waiting for transfers between devices: 54 us -> none  [the longest x1 28.4 us: local(): all_signed = lax.all_gather(signed_rows, 'ex', axis=0, tiled=True)]
    reduce_scatter x1 -> x0, waiting for transfers between devices: 31.4 us -> none  [local(): lax.psum_scatter(jnp.einsum('qf,tf->qt', everyone, train_grads, preferred...]
    dot_general x2 -> x0, matrix products: 12.7 us -> none  [the longest x1 7.36 us: local(): jnp.einsum('qf,tf->qt', everyone, train_grads, preferred_element_type=jnp...]
    reshape x1 -> x0, local copies, waits for them, and re-layouts: 2.06 us -> none  [local(): everyone = joined.reshape(joined.shape[0], lay_count * layer_width)]
    mul x2 -> x0, other arithmetic: 1.99 us -> none  [the longest x1 1.99 us: local(): signed_rows = queries * sign_flips[None, :]]
    select_n x1 -> x0, other arithmetic: 1.79 us -> none  [local(): jnp.where(query_ids[:, None] == train_ids[None, :], jnp.float32(0.0), sca...]
    unnamed x5 -> x1, local copies, waits for them, and re-layouts: 0.02 us -> 1.72 us
  transfers between devices with their start and end apart: 3 -> 0, of which waited for: 3 -> 0; matrix products, arithmetic and copies ran while one was open for 0% -> 0% of each run, Pallas kernels for 0% -> 0%
where the time goes in v1:
time: 64.1 us; the launch traced here: 63.9 us
  Pallas kernels  62.2 us (97%)
  local copies, waits for them, and re-layouts  1.72 us (3%)
    pallas_call x1, Pallas kernels, local(): pl.pallas_call(functools.partial(kernel, n_ex, n_feat), out_shape=jax.Sha...  62.2 us
    unnamed x1, local copies, waits for them, and re-layouts  1.72 us

profile of v1, /device:TPU:0, one launch (start us, length us, event | category | flops | bytes accessed | tf_op | source)
XLA Modules:
  0.0 63.9 jit_solution(13787821011558664337)
XLA Ops:
  0.0 62.2 %shard_map.64 = f32[80,1024]{1,0:T(8,128)} custom-call(bf16[80,4096]{1,0:T(8,128)(2,1)} %q_hbm.1, bf16[1024,4096]{1,0:T(8,128)(2,1)} %g_hbm.1, bf16[2,512,2048]{2,1,0:T(8,128)(2,1)} %p_hbm.1, s32[1,80]{1,0:T(1,128)} %bitcast.3, s32[1,1024]{1,0:T(1,128)} %bitcast.2, s32[2]{0:T(128)} %seed_ref.1), custom_call_target="tpu_custom_call" | custom-call | flops 4026531840 | bytes 13238272 | tf_op jit(solution)/shard_map/pallas_call | solution.py:220
  62.2 1.7 %copy.8 = f32[80,1024]{1,0:T(8,128)} copy(f32[80,1024]{1,0:T(8,128)} %shard_map.64) | data formatting | bytes 655360

commit v2 on v1

--- a/solution.py
+++ b/solution.py
@@ -9,7 +9,8 @@
 from jax.sharding import PartitionSpec as P
 
 CHUNK = 16
-TILE = 256
+AHEAD = 2
+TILE = 512
 NT = (((1,), (1,)), ((), ()))
 
 
@@ -26,7 +27,7 @@
 def kernel(
     n_ex, n_feat,
     q_hbm, g_hbm, p_hbm, qid_ref, tid_ref, seed_ref, out_ref,
-    qbuf, cbuf, gbuf, pbuf, sbuf, zbuf, own, qcol,
+    qbuf, cbuf, gbuf, pbuf, sbuf, zbuf, own, acc, qcol,
     load_q, load_p, load_g,
     q_sib_s, q_sib_r, q_y_s, q_y_r, q_fw_s, q_fw_r,
     c_sib_s, c_sib_r, c_y_s, c_y_r, c_fw_s, c_fw_r,
@@ -77,7 +78,7 @@
         for e in range(n_ex)
         for l in range(layers)
     ]
-    for copy in q_loads + p_loads + g_loads:
+    for copy in q_loads:
         copy.start()
 
     barrier = pltpu.get_barrier_semaphore()
@@ -104,6 +105,15 @@
         copy.start()
         sent.append(copy)
 
+    def send_y(i):
+        k = i % steps
+        for j in range(1, far + 1):
+            if i < steps:
+                go(remote(block(k, me), q_y_s.at[j - 1, k], q_y_r.at[j - 1, k], ahead(j)))
+            elif i < 2 * steps:
+                mine = cbuf.at[k, :, columns(me)]
+                go(remote(mine, c_y_s.at[j - 1, k], c_y_r.at[j - 1, k], ahead(j)))
+
     for k in range(steps):
         q_loads[k].wait()
         place = pl.ds(pl.multiple_of(me * CHUNK, CHUNK), CHUNK)
@@ -112,14 +122,19 @@
             qbuf[k, place, lanes] = qbuf[k, place, lanes] * signs[l]
         if k == 0:
             pl.semaphore_wait(barrier, far + n_feat)
-        for j in range(1, far + 1):
-            go(remote(block(k, me), q_y_s.at[j - 1, k], q_y_r.at[j - 1, k], ahead(j)))
+        if k < AHEAD:
+            send_y(k)
         go(remote(block(k, me), q_sib_s.at[k], q_sib_r.at[k], sib))
+
+    for copy in p_loads + g_loads:
+        copy.start()
 
     for k in range(steps):
         for j in range(1, far + 1):
             src = behind(me, j)
             remote(block(k, src), q_y_s.at[j - 1, k], q_y_r.at[j - 1, k], ahead(j)).wait_recv()
+            if j == far:
+                send_y(k + AHEAD)
             go(remote(block(k, src), q_fw_s.at[j - 1, k], q_fw_r.at[j - 1, k], sib))
         remote(block(k, sib), q_sib_s.at[k], q_sib_r.at[k], sib).wait_recv()
         for j in range(1, far + 1):
@@ -130,12 +145,10 @@
                 copy.wait()
         for l in range(layers):
             got = lax.dot_general(
-                qbuf[k, :, l * width:(l + 1) * width], pbuf[l], NT, preferred_element_type=jnp.float32
-            )
+                pbuf[l], qbuf[k, :, l * width:(l + 1) * width], NT, preferred_element_type=jnp.float32
+            ).T
             cbuf[k, :, pl.ds(pl.multiple_of(me * part + l * prow, 128), prow)] = got.astype(jnp.bfloat16)
         mine = cbuf.at[k, :, columns(me)]
-        for j in range(1, far + 1):
-            go(remote(mine, c_y_s.at[j - 1, k], c_y_r.at[j - 1, k], ahead(j)))
         go(remote(mine, c_sib_s.at[k], c_sib_r.at[k], sib))
 
     normal = 1.0 / math.sqrt(n_feat * layers * width)
@@ -167,28 +180,42 @@
             same = qcol[band, 0:1] == tid_ref[...].astype(jnp.float32)
             out_ref[band, :] = jnp.where(same, 0.0, total * normal)
 
-    for k in range(steps):
+    def product(k, lanes, tile):
+        return lax.dot_general(gbuf[tile, lanes], cbuf[k, :, lanes], NT, preferred_element_type=jnp.float32)
+
+    tiles = [slice(n * TILE, (n + 1) * TILE) for n in range(train // TILE)]
+    chip = pl.ds(pl.multiple_of((me - lax.rem(me, 2)) * part, 128), 2 * part)
+
+    for copy in g_loads:
+        copy.wait()
+    for k in range(steps):
+        remote(cbuf.at[k, :, columns(sib)], c_sib_s.at[k], c_sib_r.at[k], sib).wait_recv()
+        for tile in tiles:
+            acc[tile, :] = product(k, chip, tile)
         for j in range(1, far + 1):
             got = cbuf.at[k, :, columns(behind(me, j))]
             remote(got, c_y_s.at[j - 1, k], c_y_r.at[j - 1, k], ahead(j)).wait_recv()
+            if j == far:
+                send_y(steps + k + AHEAD)
             go(remote(got, c_fw_s.at[j - 1, k], c_fw_r.at[j - 1, k], sib))
-        remote(cbuf.at[k, :, columns(sib)], c_sib_s.at[k], c_sib_r.at[k], sib).wait_recv()
+        for j in range(1, far + 1):
+            for tile in tiles:
+                acc[tile, :] += product(k, columns(behind(me, j)), tile)
         for j in range(1, far + 1):
             got = cbuf.at[k, :, columns(behind(sib, j))]
             remote(got, c_fw_s.at[j - 1, k], c_fw_r.at[j - 1, k], sib).wait_recv()
-        if k == 0:
-            for copy in g_loads:
-                copy.wait()
-
-        for n in range(train // TILE):
-            tile = slice(n * TILE, (n + 1) * TILE)
-            scores = lax.dot_general(cbuf[k], gbuf[tile, :], NT, preferred_element_type=jnp.float32)
-            sbuf[k, :, tile] = scores.astype(jnp.bfloat16)
-            for b in range(n_ex):
-                @pl.when(fe == b // per_owner)
-                def _():
-                    spot = (b % per_owner) * steps + k
-                    own[spot * CHUNK:(spot + 1) * CHUNK, tile] = scores[b * CHUNK:(b + 1) * CHUNK]
+            for tile in tiles:
+                scores = acc[tile, :] + product(k, columns(behind(sib, j)), tile)
+                if j < far:
+                    acc[tile, :] = scores
+                    continue
+                scores = scores.T
+                sbuf[k, :, tile] = scores.astype(jnp.bfloat16)
+                for b in range(n_ex):
+                    @pl.when(fe == b // per_owner)
+                    def _():
+                        spot = (b % per_owner) * steps + k
+                        own[spot * CHUNK:(spot + 1) * CHUNK, tile] = scores[b * CHUNK:(b + 1) * CHUNK]
 
         for b in range(n_ex):
             @pl.when(fe != b // per_owner)
@@ -230,6 +257,7 @@
             pltpu.VMEM((steps, n_ex * CHUNK, train), jnp.bfloat16),
             pltpu.VMEM((n_feat, out_rows, train), jnp.bfloat16),
             pltpu.VMEM((out_rows, train), jnp.float32),
+            pltpu.VMEM((train, n_ex * CHUNK), jnp.float32),
             pltpu.VMEM((out_rows, 128), jnp.float32),
             dma((steps,)), dma((layers,)), dma((n_ex * layers,)),
             dma((steps,)), dma((steps,)), dma((far, steps)), dma((far, steps)), dma((far, steps)), dma((far, steps)),

time: 64.1 us -> 53.2 us (0.83)
  Pallas kernels: 62.2 us -> 51.3 us
    pallas_call x1, Pallas kernels: 62.2 us -> 51.3 us  [local(): pl.pallas_call(functools.partial(kernel, n_ex, n_feat), out_shape=jax.Sha...]
where the time goes in v2:
time: 53.2 us; the launch traced here: 53 us
  Pallas kernels  51.3 us (96%)
  local copies, waits for them, and re-layouts  1.72 us (3%)
    pallas_call x1, Pallas kernels, local(): pl.pallas_call(functools.partial(kernel, n_ex, n_feat), out_shape=jax.Sha...  51.3 us
    unnamed x1, local copies, waits for them, and re-layouts  1.72 us

profile of v2, /device:TPU:0, one launch (start us, length us, event | category | flops | bytes accessed | tf_op | source)
XLA Modules:
  0.0 53.0 jit_solution(2950329578051353479)
XLA Ops:
  0.0 51.3 %shard_map.64 = f32[80,1024]{1,0:T(8,128)} custom-call(bf16[80,4096]{1,0:T(8,128)(2,1)} %q_hbm.1, bf16[1024,4096]{1,0:T(8,128)(2,1)} %g_hbm.1, bf16[2,512,2048]{2,1,0:T(8,128)(2,1)} %p_hbm.1, s32[1,80]{1,0:T(1,128)} %bitcast.3, s32[1,1024]{1,0:T(1,128)} %bitcast.2, s32[2]{0:T(128)} %seed_ref.1), custom_call_target="tpu_custom_call" | custom-call | flops 4026531840 | bytes 13238272 | tf_op jit(solution)/shard_map/pallas_call | solution.py:247
  51.3 1.7 %copy.8 = f32[80,1024]{1,0:T(8,128)} copy(f32[80,1024]{1,0:T(8,128)} %shard_map.64) | data formatting | bytes 655360

commit v3 on v2

--- a/solution.py
+++ b/solution.py
@@ -9,7 +9,7 @@
 from jax.sharding import PartitionSpec as P
 
 CHUNK = 16
-AHEAD = 2
+AHEAD = 3
 TILE = 512
 NT = (((1,), (1,)), ((), ()))
 
@@ -221,9 +221,10 @@
             @pl.when(fe != b // per_owner)
             def _():
                 z_copy(k, b).start()
-        if k > 0:
-            finish(k - 1)
-    finish(steps - 1)
+        if k > 1:
+            finish(k - 2)
+    for k in range(max(steps - 2, 0), steps):
+        finish(k)
 
     for copy in sent:
         copy.wait_send()

time: 53.2 us -> 50 us (0.940)
  Pallas kernels: 51.3 us -> 48.1 us
    pallas_call x1, Pallas kernels: 51.3 us -> 48.1 us  [local(): pl.pallas_call(functools.partial(kernel, n_ex, n_feat), out_shape=jax.Sha...]
where the time goes in v3:
time: 50 us; the launch traced here: 49.8 us
  Pallas kernels  48.1 us (96%)
  local copies, waits for them, and re-layouts  1.72 us (3%)
    pallas_call x1, Pallas kernels, local(): pl.pallas_call(functools.partial(kernel, n_ex, n_feat), out_shape=jax.Sha...  48.1 us
    unnamed x1, local copies, waits for them, and re-layouts  1.72 us

profile of v3, /device:TPU:0, one launch (start us, length us, event | category | flops | bytes accessed | tf_op | source)
XLA Modules:
  0.0 49.8 jit_solution(10472264051883021827)
XLA Ops:
  0.0 48.1 %shard_map.64 = f32[80,1024]{1,0:T(8,128)} custom-call(bf16[80,4096]{1,0:T(8,128)(2,1)} %q_hbm.1, bf16[1024,4096]{1,0:T(8,128)(2,1)} %g_hbm.1, bf16[2,512,2048]{2,1,0:T(8,128)(2,1)} %p_hbm.1, s32[1,80]{1,0:T(1,128)} %bitcast.3, s32[1,1024]{1,0:T(1,128)} %bitcast.2, s32[2]{0:T(128)} %seed_ref.1), custom_call_target="tpu_custom_call" | custom-call | flops 4026531840 | bytes 13238272 | tf_op jit(solution)/shard_map/pallas_call | solution.py:248
  48.1 1.7 %copy.8 = f32[80,1024]{1,0:T(8,128)} copy(f32[80,1024]{1,0:T(8,128)} %shard_map.64) | data formatting | bytes 655360
